TPU v7x, 256 devices: a whole 4x4x8 slice. The times are simulated.
256 devices in a mesh: seq: 32 (over y_hi, z, core), tp: 8 (over y_lo, x).
Axes of the slice: x: 4, y: 4 (y_hi: 2, y_lo: 2; y = y_hi * 2 + y_lo), z: 8, core: 2. Of those that a mesh axis runs over, the one named last changes fastest.
Arguments:
- prompt: bfloat16 [4096, 5376], P(('seq', 'tp'))
- answers: bfloat16 [32, 64, 5376], P('seq', 'tp')
- answer_lengths: int32 [32], P('seq'), may hold values from 1 to 64, as said below
- input_gain: float32 [5376], replicated, may hold values from 0.1 to 1.9
- query_weight: bfloat16 [5376, 4096], P('seq', 'tp'), may hold values from -0.078125 to 0.078125
- key_weight: bfloat16 [5376, 2048], P('seq', 'tp'), may hold values from -0.078125 to 0.078125
- value_weight: bfloat16 [5376, 2048], P('seq', 'tp'), may hold values from -0.078125 to 0.078125
- query_gain: float32 [128], replicated, may hold values from 0.1 to 1.9
- key_gain: float32 [128], replicated, may hold values from 0.1 to 1.9
- out_weight: bfloat16 [4096, 5376], P(('tp', 'seq')), may hold values from -0.09375 to 0.09375
- post_gain: float32 [5376], replicated, may hold values from 0.1 to 1.9
Outputs:
- prompt_out: bfloat16 [4096, 5376], P(('seq', 'tp'))
- answer_out: bfloat16 [32, 64, 5376], P('seq', 'tp')
Inputs may be any that keep to these rules, and one draw needn't show every extreme that they name: `answer_lengths`: some candidate has 64 live tokens and some has 1.
All inputs are finite; a program needn't handle non-finite values.
Results may differ from a plain program's by a relative error of at most 0.015.
Values may be sent and summed in bfloat16 or wider, within the bound.
A program may use at most 64 MiB of HBM per device.

v0:
```python
import jax
import jax.numpy as jnp
from jax import lax
from jax.sharding import PartitionSpec as P

HEAD_DIM = 128
WINDOW = 1024


epsilon = 1e-06
query_scale = 168.0 ** (-0.5)


def passed_along(value, axis, by):
    peers = lax.axis_size(axis)
    pairs = [(i, i + by) for i in range(peers) if 0 <= i + by < peers]
    return lax.ppermute(value, axis, pairs)


def broadcast(block, axis, holder):
    block = jnp.where(lax.axis_index(axis) == holder, block, jnp.zeros_like(block))
    return lax.psum(block, axis)


def rms_norm(inputs, gains):
    mean_square = jnp.mean(inputs * inputs, axis=-1, keepdims=True)
    return inputs * lax.rsqrt(mean_square + epsilon) * gains


def attend(query_rows, key_rows, value_rows, visible):
    row_count = query_rows.shape[0]
    outputs = []
    for head_index in range(key_rows.shape[1]):
        scores = jnp.einsum(
            "ngd,md->gnm",
            query_rows[:, head_index],
            key_rows[:, head_index],
            preferred_element_type=jnp.float32,
        )
        weights = jnp.where(visible[None], jnp.exp(scores), 0.0)
        totals = jnp.sum(weights, axis=-1)
        summed = jnp.einsum(
            "gnm,md->ngd",
            weights.astype(jnp.bfloat16),
            value_rows[:, head_index],
            preferred_element_type=jnp.float32,
        )
        outputs.append(summed / jnp.transpose(totals)[:, :, None])
    return jnp.stack(outputs, 1).reshape(row_count, -1).astype(jnp.bfloat16)


def on_device(
    prompt,
    answers,
    answer_lengths,
    input_gain,
    query_weight,
    key_weight,
    value_weight,
    query_gain,
    key_gain,
    out_weight,
    post_gain,
):
    tp_size = lax.axis_size("tp")
    seq_size = lax.axis_size("seq")
    seq_index = lax.axis_index("seq")
    tp_index = lax.axis_index("tp")
    tok_dev = prompt.shape[0] * tp_size
    cand_dev = answers.shape[0]
    ans_part = answers.shape[1]
    ans_len = ans_part * tp_size
    width = answers.shape[2]
    reach = WINDOW // tok_dev
    local_heads = query_weight.shape[1] // HEAD_DIM
    local_groups = key_weight.shape[1] // HEAD_DIM
    group_size = local_heads // local_groups
    prompt_full, answer_full = (
        lax.all_gather(prompt[None], "tp", axis=1, tiled=True),
        lax.all_gather(answers, "tp", axis=1, tiled=True),
    )
    stacked = jnp.concatenate([prompt_full[0], answer_full.reshape(cand_dev * ans_len, width)], 0)
    total_rows = stacked.shape[0]
    normed = rms_norm(stacked.astype(jnp.float32), input_gain).astype(jnp.bfloat16)

    def project_in(weight_full):
        return jnp.dot(normed, weight_full, preferred_element_type=jnp.float32)

    query_full, key_full, value_full = (
        lax.all_gather(query_weight, "seq", axis=0, tiled=True),
        lax.all_gather(key_weight, "seq", axis=0, tiled=True),
        lax.all_gather(value_weight, "seq", axis=0, tiled=True),
    )
    query_raw = project_in(query_full)
    key_rows = rms_norm(
        project_in(key_full).reshape(total_rows, local_groups, HEAD_DIM), key_gain
    ).astype(jnp.bfloat16)
    value_rows = (
        project_in(value_full).astype(jnp.bfloat16).reshape(total_rows, local_groups, HEAD_DIM)
    )
    key_rows, value_rows = (key_rows, value_rows)
    own_pair = jnp.stack(
        [key_rows[:tok_dev].reshape(tok_dev, -1), value_rows[:tok_dev].reshape(tok_dev, -1)]
    )
    received = [passed_along(own_pair, "seq", reach - offset) for offset in range(reach)]
    extended = jnp.concatenate(received + [own_pair], 1)
    window_pair = broadcast(extended[:, tok_dev:], "seq", seq_size - 1)
    extended, window_pair = (extended, window_pair)
    query_rows = (
        rms_norm(query_raw.reshape(total_rows, local_heads, HEAD_DIM), query_gain) * query_scale
    ).astype(jnp.bfloat16)
    query_rows = query_rows.reshape(total_rows, local_groups, group_size, HEAD_DIM)
    output_full = lax.all_gather(out_weight, "seq", axis=0, tiled=True)
    prompt_keys = extended[0].reshape(-1, local_groups, HEAD_DIM)
    prompt_values = extended[1].reshape(-1, local_groups, HEAD_DIM)
    query_pos = seq_index * tok_dev + jnp.arange(tok_dev, dtype=jnp.int32)
    key_pos = (seq_index - reach) * tok_dev + jnp.arange((reach + 1) * tok_dev, dtype=jnp.int32)
    prompt_visible = (
        (key_pos[None, :] >= 0)
        & (key_pos[None, :] <= query_pos[:, None])
        & (key_pos[None, :] > query_pos[:, None] - WINDOW)
    )
    prompt_attention = attend(query_rows[:tok_dev], prompt_keys, prompt_values, prompt_visible)
    window_keys = window_pair[0].reshape(WINDOW, local_groups, HEAD_DIM)
    window_values = window_pair[1].reshape(WINDOW, local_groups, HEAD_DIM)
    answer_pos = jnp.arange(ans_len, dtype=jnp.int32)[:, None]
    window_seen = jnp.arange(WINDOW, dtype=jnp.int32)[None, :] > answer_pos
    own_seen = jnp.arange(ans_len, dtype=jnp.int32)[None, :] <= answer_pos
    answer_visible = jnp.concatenate([window_seen, own_seen], 1)

    def answer_block(items):
        cand_queries, cand_keys, cand_values = items
        all_keys = jnp.concatenate([window_keys, cand_keys], 0)
        all_values = jnp.concatenate([window_values, cand_values], 0)
        return attend(cand_queries, all_keys, all_values, answer_visible)

    answer_attention = lax.map(
        answer_block,
        (
            query_rows[tok_dev:].reshape(cand_dev, ans_len, local_groups, group_size, HEAD_DIM),
            key_rows[tok_dev:].reshape(cand_dev, ans_len, local_groups, HEAD_DIM),
            value_rows[tok_dev:].reshape(cand_dev, ans_len, local_groups, HEAD_DIM),
        ),
    )
    answer_flat = answer_attention.reshape(cand_dev * ans_len, -1)
    mixed = jnp.dot(
        jnp.concatenate([prompt_attention, answer_flat], 0),
        output_full,
        preferred_element_type=jnp.float32,
    )
    prompt_share, answer_share = (
        lax.psum_scatter(
            mixed[:tok_dev][None].astype(jnp.bfloat16), "tp", scatter_dimension=1, tiled=True
        ).astype(jnp.float32),
        lax.psum_scatter(
            mixed[tok_dev:].reshape(cand_dev, ans_len, width).astype(jnp.bfloat16),
            "tp",
            scatter_dimension=1,
            tiled=True,
        ).astype(jnp.float32),
    )
    prompt_out = (prompt.astype(jnp.float32) + rms_norm(prompt_share[0], post_gain)).astype(
        jnp.bfloat16
    )
    answer_sum = answers.astype(jnp.float32) + rms_norm(answer_share, post_gain)
    positions = tp_index * ans_part + jnp.arange(ans_part, dtype=jnp.int32)
    live = positions[None, :] < answer_lengths[:, None]
    answer_out = jnp.where(live[:, :, None], answer_sum, 0.0).astype(jnp.bfloat16)
    return (prompt_out, answer_out)


def solution(mesh):
    placed = (
        P(("seq", "tp"), None),
        P("seq", "tp", None),
        P("seq"),
        P(),
        P("seq", "tp"),
        P("seq", "tp"),
        P("seq", "tp"),
        P(),
        P(),
        P(("tp", "seq"), None),
        P(),
    )
    return jax.shard_map(
        on_device,
        mesh=mesh,
        in_specs=placed,
        out_specs=(P(("seq", "tp"), None), P("seq", "tp", None)),
        check_vma=False,
    )
```

profile of v0, /device:TPU:1, one launch (start us, length us, event | category | flops | bytes accessed | tf_op | source)
XLA Modules:
  0.0 818.9 jit_solution(13781233932783436836)
XLA Ops:
  9.4 26.0 %all_gather.19 = bf16[1,64,5376]{2,1,0:T(8,128)(2,1)S(1)} all-gather(bf16[1,8,5376]{2,1,0:T(8,128)(2,1)} %param.12), channel_id=1, replica_groups=mesh['seq'=32,'tp'=8] {'tp'}, dimensions={1}, use_global_device_ids=true | all-gather | bytes 774144 | tf_op jit(solution)/shard_map/all_gather | solution.py:80
  35.5 16.5 %all-gather.15.cloned.1.call-done = bf16[128,5376]{1,0:T(8,128)(2,1)} async-done(((bf16[16,5376]{1,0:T(8,128)(2,1)}), bf16[128,5376]{1,0:T(8,128)(2,1)}) %all-gather.15.cloned.1.call-update) | async-done | bytes 1376272 | tf_op jit(solution)/shard_map/all_gather | solution.py:79
  52.0 1.9 fusion
  53.9 87.7 %all-gather.7.cloned.1.call-done = bf16[5376,256]{1,0:T(8,128)(2,1)} async-done(((bf16[168,256]{1,0:T(8,128)(2,1)}), bf16[5376,256]{1,0:T(8,128)(2,1)}) %all-gather.7.cloned.1.call-update) | async-done | bytes 2752528 | tf_op jit(solution)/shard_map/all_gather | solution.py:91
  141.7 2.5 fusion.53
  145.0 78.3 %all-gather.9.cloned.1.call-done = bf16[5376,256]{1,0:T(8,128)(2,1)} async-done(((bf16[168,256]{1,0:T(8,128)(2,1)}), bf16[5376,256]{1,0:T(8,128)(2,1)}) %all-gather.9.cloned.1.call-update) | async-done | bytes 2752528 | tf_op jit(solution)/shard_map/all_gather | solution.py:92
  223.3 2.5 convolution_convert_fusion.1
  225.9 4.7 collective-permute-start
  230.6 4.8 collective-permute-start.1
  235.4 4.6 collective-permute-start.2
  240.0 3.2 collective-permute-start.3
  243.3 2.6 collective-permute-start.4
  245.9 2.1 collective-permute-start.5
  248.7 2.4 collective-permute-start.6
  251.8 6.9 collective-permute-start.7
  261.6 7.6 collective-permute-done.5
  269.9 2.1 collective-permute-done.6
  278.0 1.3 fusion.55
  280.6 1.6 fusion.57
  282.2 261.3 %all-reduce.2.cloned.1.call-done = bf16[2,1024,256]{2,1,0:T(8,128)(2,1)} async-done(((bf16[2,1024,256]{2,1,0:T(8,128)(2,1)}), bf16[2,1024,256]{2,1,0:T(8,128)(2,1)}) %all-reduce.2.cloned.1.call-update) | async-done | bytes 1048592 | tf_op jit(solution)/shard_map/psum | solution.py:22
  543.5 1.3 fusion.56
  547.4 89.6 %all-gather.11.cloned.1.call-done = bf16[5376,512]{1,0:T(8,128)(2,1)} async-done(((bf16[168,512]{1,0:T(8,128)(2,1)}), bf16[5376,512]{1,0:T(8,128)(2,1)}) %all-gather.11.cloned.1.call-update) | async-done | bytes 5505040 | tf_op jit(solution)/shard_map/all_gather | solution.py:90
  637.1 3.8 fusion.50
  642.3 1.2 fusion.22
  643.9 1.2 fusion.21
  646.8 81.5 %all-gather.13.cloned.1.call-done = bf16[512,5376]{1,0:T(8,128)(2,1)} async-done(((bf16[16,5376]{1,0:T(8,128)(2,1)}), bf16[512,5376]{1,0:T(8,128)(2,1)}) %all-gather.13.cloned.1.call-update) | async-done | bytes 5505040 | tf_op jit(solution)/shard_map/all_gather | solution.py:113
  728.2 3.8 convolution_convert_fusion
  733.1 1.2 slice_bitcast_fusion
  735.0 29.9 %reduce-scatter.5.cloned.1.call-done = bf16[1,8,5376]{2,1,0:T(8,128)(2,1)} async-done(((bf16[1,64,5376]{2,1,0:T(8,128)(2,1)}), bf16[1,8,5376]{2,1,0:T(8,128)(2,1)}) %reduce-scatter.5.cloned.1.call-update) | async-done | bytes 86032 | tf_op jit(solution)/shard_map/reduce_scatter | solution.py:155
  765.9 1.6 fusion.46
  767.6 41.7 %reduce-scatter.3.cloned.1.call-done = bf16[1,16,5376]{2,1,0:T(8,128)(2,1)} async-done(((bf16[1,128,5376]{2,1,0:T(8,128)(2,1)}), bf16[1,16,5376]{2,1,0:T(8,128)(2,1)}) %reduce-scatter.3.cloned.1.call-update) | async-done | bytes 172048 | tf_op jit(solution)/shard_map/reduce_scatter | solution.py:152
  810.3 1.7 fusion.28
  (105 shorter events, 24.1 us)
Async XLA Ops:
  7.2 134.5 %copy-start.11 = (f32[5376]{0:T(1024)S(1)}, f32[5376]{0:T(1024)}, u32[]{:S(2)}) copy-start(f32[5376]{0:T(1024)} %param.14) | copy-start | bytes 64516
  7.2 44.8 %all-gather.15.cloned.1.call-start = ((), (), s32[]{:S(2)}) async-start(), calls=%async_computation.9 | async-start | bytes 1548288 | tf_op jit(solution)/shard_map/all_gather | solution.py:79
  7.9 133.8 %all-gather.7.cloned.1.call-start = ((), (), s32[]{:S(2)}) async-start(), calls=%async_computation.2 | async-start | bytes 2838528 | tf_op jit(solution)/shard_map/all_gather | solution.py:91
  8.7 214.6 %all-gather.9.cloned.1.call-start = ((), (), s32[]{:S(2)}) async-start(), calls=%async_computation.3 | async-start | bytes 2838528 | tf_op jit(solution)/shard_map/all_gather | solution.py:92
  9.4 534.2 %all-reduce.2.cloned.1.call-start = ((), (), s32[]{:S(2)}) async-start(), calls=%async_computation.5 | async-start | bytes 2097152 | tf_op jit(solution)/shard_map/psum | solution.py:22
  52.0 89.7 %copy-start = (bf16[128,5376]{1,0:T(8,128)(2,1)S(1)}, bf16[128,5376]{1,0:T(8,128)(2,1)}, u32[]{:S(2)}) copy-start(bf16[128,5376]{1,0:T(8,128)(2,1)} %all-gather.15.cloned.1.call-done) | copy-start | bytes 4128772
  53.9 90.7 %copy-start.9 = (f32[128]{0:T(128)S(1)}, f32[128]{0:T(128)}, u32[]{:S(2)}) copy-start(f32[128]{0:T(128)} %param.19) | copy-start | bytes 1540
  225.9 20.0 %collective-permute-start = (bf16[2,128,256]{2,1,0:T(8,128)(2,1)S(1)}, bf16[2,128,256]{2,1,0:T(8,128)(2,1)S(1)}, u32[]{:S(2)}, u32[]{:S(2)}) collective-permute-start(bf16[2,128,256]{2,1,0:T(8,128)(2,1)S(1)} %pad_maximum_fusion.2), channel_id=1, source_target_pairs={{0,64},{8,72},{16,80},{24,88},{32,96},{40,104},{48,112},{56,120},{... | collective-permute-start | bytes 393224 | tf_op jit(solution)/shard_map/ppermute | solution.py:17
  230.6 18.1 %collective-permute-start.1 = (bf16[2,128,256]{2,1,0:T(8,128)(2,1)S(1)}, bf16[2,128,256]{2,1,0:T(8,128)(2,1)S(1)}, u32[]{:S(2)}, u32[]{:S(2)}) collective-permute-start(bf16[2,128,256]{2,1,0:T(8,128)(2,1)S(1)} %pad_maximum_fusion.2), channel_id=1, source_target_pairs={{0,56},{8,64},{16,72},{24,80},{32,88},{40,96},{48,104},{56,112},{6... | collective-permute-start | bytes 393224 | tf_op jit(solution)/shard_map/ppermute | solution.py:17
  235.4 16.4 %collective-permute-start.2 = (bf16[2,128,256]{2,1,0:T(8,128)(2,1)S(1)}, bf16[2,128,256]{2,1,0:T(8,128)(2,1)S(1)}, u32[]{:S(2)}, u32[]{:S(2)}) collective-permute-start(bf16[2,128,256]{2,1,0:T(8,128)(2,1)S(1)} %pad_maximum_fusion.2), channel_id=1, source_target_pairs={{0,48},{8,56},{16,64},{24,72},{32,80},{40,88},{48,96},{56,104},{64... | collective-permute-start | bytes 393224 | tf_op jit(solution)/shard_map/ppermute | solution.py:17
  240.0 19.3 %collective-permute-start.3 = (bf16[2,128,256]{2,1,0:T(8,128)(2,1)S(1)}, bf16[2,128,256]{2,1,0:T(8,128)(2,1)S(1)}, u32[]{:S(2)}, u32[]{:S(2)}) collective-permute-start(bf16[2,128,256]{2,1,0:T(8,128)(2,1)S(1)} %pad_maximum_fusion.2), channel_id=1, source_target_pairs={{0,40},{8,48},{16,56},{24,64},{32,72},{40,80},{48,88},{56,96},{64,... | collective-permute-start | bytes 393224 | tf_op jit(solution)/shard_map/ppermute | solution.py:17
  243.3 17.7 %collective-permute-start.4 = (bf16[2,128,256]{2,1,0:T(8,128)(2,1)S(1)}, bf16[2,128,256]{2,1,0:T(8,128)(2,1)S(1)}, u32[]{:S(2)}, u32[]{:S(2)}) collective-permute-start(bf16[2,128,256]{2,1,0:T(8,128)(2,1)S(1)} %pad_maximum_fusion.2), channel_id=1, source_target_pairs={{0,32},{8,40},{16,48},{24,56},{32,64},{40,72},{48,80},{56,88},{64,... | collective-permute-start | bytes 393224 | tf_op jit(solution)/shard_map/ppermute | solution.py:17
  245.9 23.3 %collective-permute-start.5 = (bf16[2,128,256]{2,1,0:T(8,128)(2,1)S(1)}, bf16[2,128,256]{2,1,0:T(8,128)(2,1)S(1)}, u32[]{:S(2)}, u32[]{:S(2)}) collective-permute-start(bf16[2,128,256]{2,1,0:T(8,128)(2,1)S(1)} %pad_maximum_fusion.2), channel_id=1, source_target_pairs={{0,24},{8,32},{16,40},{24,48},{32,56},{40,64},{48,72},{56,80},{64,... | collective-permute-start | bytes 393224 | tf_op jit(solution)/shard_map/ppermute | solution.py:17
  248.7 23.2 %collective-permute-start.6 = (bf16[2,128,256]{2,1,0:T(8,128)(2,1)S(1)}, bf16[2,128,256]{2,1,0:T(8,128)(2,1)S(1)}, u32[]{:S(2)}, u32[]{:S(2)}) collective-permute-start(bf16[2,128,256]{2,1,0:T(8,128)(2,1)S(1)} %pad_maximum_fusion.2), channel_id=1, source_target_pairs={{0,16},{8,24},{16,32},{24,40},{32,48},{40,56},{48,64},{56,72},{64,... | collective-permute-start | bytes 393224 | tf_op jit(solution)/shard_map/ppermute | solution.py:17
  251.8 21.6 %collective-permute-start.7 = (bf16[2,128,256]{2,1,0:T(8,128)(2,1)S(1)}, bf16[2,128,256]{2,1,0:T(8,128)(2,1)S(1)}, u32[]{:S(2)}, u32[]{:S(2)}) collective-permute-start(bf16[2,128,256]{2,1,0:T(8,128)(2,1)S(1)} %pad_maximum_fusion.2), channel_id=1, source_target_pairs={{0,8},{8,16},{16,24},{24,32},{32,40},{40,48},{48,56},{56,64},{64,7... | collective-permute-start | bytes 393224 | tf_op jit(solution)/shard_map/ppermute | solution.py:17
  275.8 361.3 %all-gather.11.cloned.1.call-start = ((), (), s32[]{:S(2)}) async-start(), calls=%async_computation.4 | async-start | bytes 5677056 | tf_op jit(solution)/shard_map/all_gather | solution.py:90
  276.4 451.8 %all-gather.13.cloned.1.call-start = ((), (), s32[]{:S(2)}) async-start(), calls=%async_computation.6 | async-start | bytes 5677056 | tf_op jit(solution)/shard_map/all_gather | solution.py:113
  277.0 487.9 %reduce-scatter.5.cloned.1.call-start = ((), (), s32[]{:S(2)}) async-start(), calls=%async_computation.8 | async-start | bytes 774144 | tf_op jit(solution)/shard_map/reduce_scatter | solution.py:155
  544.9 92.1 %copy-start.1 = (bf16[128,5376]{1,0:T(8,128)(2,1)S(1)}, bf16[128,5376]{1,0:T(8,128)(2,1)}, u32[]{:S(2)}) copy-start(bf16[128,5376]{1,0:T(8,128)(2,1)} %all-gather.15.cloned.1.call-done) | copy-start | bytes 4128772
  547.4 93.9 %copy-start.10 = (f32[128]{0:T(128)S(1)}, f32[128]{0:T(128)}, u32[]{:S(2)}) copy-start(f32[128]{0:T(128)} %param.18) | copy-start | bytes 1540
  640.9 1.0 copy-start.6
  642.0 3.3 copy-start.5
  643.5 2.2 copy-start.3
  643.9 2.1 copy-start.4
  733.0 32.9 %copy-start.7 = (bf16[1,8,5376]{2,1,0:T(8,128)(2,1)S(1)}, bf16[1,8,5376]{2,1,0:T(8,128)(2,1)}, u32[]{:S(2)}) copy-start(bf16[1,8,5376]{2,1,0:T(8,128)(2,1)} %param.12) | copy-start | bytes 258052
  733.0 32.9 %copy-start.8 = (f32[5376]{0:T(1024)S(1)}, f32[5376]{0:T(1024)}, u32[]{:S(2)}) copy-start(f32[5376]{0:T(1024)} %param.21) | copy-start | bytes 64516
  733.0 77.3 %copy-start.2 = (bf16[16,5376]{1,0:T(8,128)(2,1)S(1)}, bf16[16,5376]{1,0:T(8,128)(2,1)}, u32[]{:S(2)}) copy-start(bf16[16,5376]{1,0:T(8,128)(2,1)} %param.11) | copy-start | bytes 516100
  733.0 76.2 %reduce-scatter.3.cloned.1.call-start = ((), (), s32[]{:S(2)}) async-start(), calls=%async_computation.7 | async-start | bytes 1548288 | tf_op jit(solution)/shard_map/reduce_scatter | solution.py:152
Sparse Core Ops, SparseCore 0:
  9.8 42.1 all-gather.14
  54.7 86.9 all-gather.6
  144.4 78.8 all-gather.8
  275.9 267.5 all-reduce.1
  546.6 90.4 all-gather.10
  640.1 88.1 all-gather.12
  733.1 31.6 reduce-scatter.4
  767.6 41.6 reduce-scatter.2
where the time goes:
time: 823 us; the launch traced here: 819 us
  waiting for transfers between devices  701 us (85%)
  starting transfers between devices  31.7 us (4%)
  blocking collectives  26 us (3%)
  matrix products  17.2 us (2%)
  local copies, waits for them, and re-layouts  16.4 us (2%)
  between operations  15.3 us (2%)
  other arithmetic  11.1 us (1%)
    psum x1, waiting for transfers between devices, broadcast(): return lax.psum(block, axis)  261 us
    all_gather x1, waiting for transfers between devices, on_device(): lax.all_gather(query_weight, 'seq', axis=0, tiled=True)  89.6 us
    all_gather x1, waiting for transfers between devices, on_device(): lax.all_gather(key_weight, 'seq', axis=0, tiled=True)  87.7 us
    all_gather x1, waiting for transfers between devices, on_device(): output_full = lax.all_gather(out_weight, 'seq', axis=0, tiled=True)  81.5 us
    all_gather x1, waiting for transfers between devices, on_device(): lax.all_gather(value_weight, 'seq', axis=0, tiled=True)  78.3 us
    reduce_scatter x1, waiting for transfers between devices, on_device(): lax.psum_scatter(mixed[:tok_dev][None].astype(jnp.bfloat16), 'tp', scatte...  41.7 us
    ppermute x8, starting transfers between devices, passed_along(): return lax.ppermute(value, axis, pairs)  31.4 us
    reduce_scatter x1, waiting for transfers between devices, on_device(): lax.psum_scatter(mixed[tok_dev:].reshape(cand_dev, ans_len, width).astype...  29.9 us
  transfers between devices with their start and end apart: 16, of which 12 were waited for; matrix products, arithmetic and copies ran while one was open for 4% of the time, Pallas kernels for 0%

commit v1 on v0

v1 whole, which is shorter than its diff:
```python
import jax
import jax.numpy as jnp
from jax import lax
from jax.experimental import pallas as pl
from jax.experimental.pallas import tpu as pltpu
from jax.sharding import PartitionSpec as P

D = 5376
HALF = D // 2
HEAD = 128
ROWS_W = 168
PAIR_W = 2 * ROWS_W
PAD_W = 176
EPS = 1e-06
QUERY_SCALE = 168.0 ** (-0.5)
KC = 384

bf16 = jnp.bfloat16
f32 = jnp.float32

AG = ((0, 640, "x"), (640, 640, "y"), (1280, 640, "x"), (1920, 768, "y"))
RS = (
    (0, 512, "x"),
    (512, 512, "y"),
    (1024, 512, "x"),
    (1536, 512, "y"),
    (2048, 256, "x"),
    (2304, 384, "y"),
)
ORDER = (1, 3, 2)


def kernel(
    prompt,
    answers,
    lens,
    in_gain,
    wq,
    wk,
    wv,
    q_gain,
    k_gain,
    wo,
    post_gain,
    p_out,
    a_out,
    st,
    rx,
    wg,
    xg,
    acc,
    kvg,
    akv,
    qp,
    qa,
    num,
    tot,
    att,
    og,
    sb,
    r1,
    s2,
    r2,
    mix,
    e_ss,
    e_rs,
    w_ss,
    w_rs,
    o_ss,
    o_rs,
    kv_ss,
    kv_rs,
    ag_ss,
    ag_rs,
    r1_ss,
    r1_rs,
    r2_ss,
    r2_rs,
):
    seq = lax.axis_index("seq")
    tp = lax.axis_index("tp")
    yh, z, c = seq // 16, (seq // 2) % 8, seq % 2
    yl, x = tp // 4, tp % 4
    y = yh * 2 + yl

    def dev(y_, x_, z_, c_):
        return ((y_ // 2) * 16 + z_ * 2 + c_, (y_ % 2) * 4 + x_)

    sib = dev(y, x, z, 1 - c)
    z_fwd = dev(y, x, (z + 1) % 8, c)
    z_bwd = dev(y, x, (z + 7) % 8, c)
    diag = dev((y + 2) % 4, x, z, 1 - c)

    def peer(axis, d):
        if axis == "x":
            return dev(y, (x + d) % 4, z, c)
        return dev((y + d) % 4, x, z, c)

    partners = [sib, z_fwd, z_bwd, diag] + [peer(a, d) for a in "xy" for d in ORDER]
    barrier = pltpu.get_barrier_semaphore()
    for target in partners:
        pl.semaphore_signal(
            barrier, inc=1, device_id=target, device_id_type=pl.DeviceIdType.MESH
        )

    started = []

    def send(src, dst, send_sem, recv_sem, target):
        copy = pltpu.make_async_remote_copy(
            src_ref=src,
            dst_ref=dst,
            send_sem=send_sem,
            recv_sem=recv_sem,
            device_id=target,
            device_id_type=pl.DeviceIdType.MESH,
        )
        copy.start()
        started.append(copy)

    def arrived(dst, send_sem, recv_sem):
        pltpu.make_async_remote_copy(
            src_ref=dst,
            dst_ref=dst,
            send_sem=send_sem,
            recv_sem=recv_sem,
            device_id=sib,
            device_id_type=pl.DeviceIdType.MESH,
        ).wait_recv()

    for h in range(2):
        st[h, 0, :ROWS_W, :] = wq[:, 256 * h : 256 * h + 256]
        st[h, 1, :ROWS_W, :128] = wk[:, 128 * h : 128 * h + 128]
        st[h, 1, :ROWS_W, 128:] = wv[:, 128 * h : 128 * h + 128]
    pl.semaphore_wait(barrier, len(partners))
    send(st.at[yh, 1 - c], rx.at[0], e_ss.at[0], e_rs.at[0], sib)
    send(st.at[1 - yh, c], rx.at[1], e_ss.at[1], e_rs.at[1], peer("y", 2))
    send(st.at[1 - yh, 1 - c], rx.at[2], e_ss.at[2], e_rs.at[2], diag)

    gain = in_gain[...]
    rows = prompt[...].astype(f32)
    rows = rows * lax.rsqrt(jnp.mean(rows * rows, axis=-1, keepdims=True) + EPS) * gain
    xg[y, x, 0:16, :] = rows[:, :HALF].astype(bf16)
    xg[y, x, 16:32, :] = rows[:, HALF:].astype(bf16)
    rows = answers[...].astype(f32)
    rows = rows * lax.rsqrt(jnp.mean(rows * rows, axis=-1, keepdims=True) + EPS) * gain
    xg[y, x, 32:48, :] = jnp.concatenate([rows[:, :HALF], rows[:, HALF:]], 0).astype(bf16)

    def ag_one(q, y_, x_):
        start, width, _ = AG[q]
        return xg.at[y_, x_, :, pl.ds(start, width)]

    def ag_line(q, k):
        start, width, axis = AG[q]
        if axis == "x":
            return xg.at[k, :, :, pl.ds(start, width)]
        return xg.at[:, k, :, pl.ds(start, width)]

    def ag_first(q):
        axis = AG[q][2]
        for d in ORDER:
            send(
                ag_one(q, y, x),
                ag_one(q, y, x),
                ag_ss.at[q, 0, d - 1],
                ag_rs.at[q, 0, d - 1],
                peer(axis, d),
            )

    def ag_second(q):
        axis = AG[q][2]
        for d in ORDER:
            if axis == "x":
                piece = ag_one(q, y, (x + 4 - d) % 4)
            else:
                piece = ag_one(q, (y + 4 - d) % 4, x)
            arrived(piece, ag_ss.at[q, 0, d - 1], ag_rs.at[q, 0, d - 1])
        mine = ag_line(q, y if axis == "x" else x)
        for d in ORDER:
            send(
                mine,
                mine,
                ag_ss.at[q, 1, d - 1],
                ag_rs.at[q, 1, d - 1],
                peer("y" if axis == "x" else "x", d),
            )

    def ag_done(q):
        axis = AG[q][2]
        own = y if axis == "x" else x
        for d in ORDER:
            arrived(
                ag_line(q, (own + 4 - d) % 4), ag_ss.at[q, 1, d - 1], ag_rs.at[q, 1, d - 1]
            )

    for q in range(len(AG)):
        ag_first(q)

    def w_block(core, m):
        return wg.at[core, pl.ds(pl.multiple_of(m * PAIR_W, 16), PAIR_W), :]

    def w_index(h, dz):
        return ((yh + h) % 2) * 8 + (z + dz) % 8

    def w_send(m, way, target):
        send(w_block(c, m), w_block(c, m), w_ss.at[way, m], w_rs.at[c, m], target)

    def pair_up(h, mine, other):
        low = jnp.where(c == 0, mine, other)
        high = jnp.where(c == 0, other, mine)
        m = w_index(h, 0)
        wg[c, pl.ds(pl.multiple_of(m * PAIR_W, 16), PAIR_W), :] = jnp.concatenate(
            [low, high], 0
        ).astype(bf16)
        w_send(m, 0, z_fwd)
        w_send(m, 1, z_bwd)
        w_send(m, 2, sib)

    arrived(rx.at[0], e_ss.at[0], e_rs.at[0])
    pair_up(
        0,
        st[yh, c, :ROWS_W, :].astype(f32),
        rx[0, :ROWS_W, :].astype(f32),
    )
    arrived(rx.at[1], e_ss.at[1], e_rs.at[1])
    arrived(rx.at[2], e_ss.at[2], e_rs.at[2])
    pair_up(1, rx[1, :ROWS_W, :].astype(f32), rx[2, :ROWS_W, :].astype(f32))

    def w_pass(h, k, way):
        m = w_index(h, 8 - k if way == 0 else k)
        arrived(w_block(c, m), w_ss.at[2, m], w_rs.at[c, m])
        if k < (4 if h == way else 3):
            w_send(m, way, z_fwd if way == 0 else z_bwd)
        w_send(m, 2, sib)

    def w_step(k):
        for h in range(2):
            for way in range(2):
                if k <= (4 if h == way else 3):
                    w_pass(h, k, way)

    def o_send(slot, way, target):
        send(og.at[slot], og.at[slot], o_ss.at[way, slot], o_rs.at[slot], target)

    def o_start():
        slot = z * 2 + c
        og[slot] = wo[...]
        o_send(slot, 0, z_fwd)
        o_send(slot, 1, z_bwd)
        o_send(slot, 2, sib)

    def o_step(k):
        for way in range(2):
            reach = 3 if way == 0 else 4
            if k <= reach:
                slot = ((z + (8 - k if way == 0 else k)) % 8) * 2 + c
                arrived(og.at[slot], o_ss.at[2, slot], o_rs.at[slot])
                if k < reach:
                    o_send(slot, way, z_fwd if way == 0 else z_bwd)
                o_send(slot, 2, sib)

    for q in range(len(AG)):
        ag_second(q)
    for k in range(1, 5):
        w_step(k)
        if k == 3:
            o_start()
    for q in range(len(AG)):
        ag_done(q)
    for m in range(16):
        arrived(w_block(1 - c, m), w_ss.at[2, m], w_rs.at[1 - c, m])

    def project(core):
        acc[...] = jnp.zeros_like(acc)
        for h in range(2):

            def body(i, carry):
                cols = pl.ds(pl.multiple_of(i * KC, 128), KC)
                ask = xg[:, :, 16 * h : 16 * h + 16, cols].reshape(256, KC)
                tail = xg[:, :, 32:48, cols].astype(f32)
                tail = tail[:, :, 8 * h : 8 * h + 8, :].reshape(128, KC).astype(bf16)
                krows = pl.ds(pl.multiple_of(h * HALF + i * KC, 128), KC)
                acc[...] += jnp.dot(
                    jnp.concatenate([ask, tail], 0),
                    wg[core, krows, :],
                    preferred_element_type=f32,
                )
                return carry

            lax.fori_loop(0, HALF // KC, body, 0)

    def head_norm(raw, gains):
        return raw * lax.rsqrt(jnp.mean(raw * raw, axis=-1, keepdims=True) + EPS) * gains

    o_step(1)
    project(1)
    keys = head_norm(acc[:, :128], k_gain[...]).astype(bf16)
    values = acc[:, 128:].astype(bf16)
    for g in range(2):
        kvg[g, z, c, :, :128] = keys[g * 128 : (g + 1) * 128]
        kvg[g, z, c, :, 128:] = values[g * 128 : (g + 1) * 128]
    akv[:, :128] = keys[256:]
    akv[:, 128:] = values[256:]

    def kv_send(g, zs, way, target):
        piece = kvg.at[g, zs, c]
        send(piece, piece, kv_ss.at[way, g, zs], kv_rs.at[g, zs, c], target)

    for g in range(2):
        kv_send(g, z, 0, z_fwd)
        kv_send(g, z, 2, sib)
    kv_send(1, z, 1, z_bwd)

    o_step(2)
    project(0)
    for h in range(2):
        raw = acc[:, 128 * h : 128 * h + 128]
        normed = (head_norm(raw, q_gain[...]) * QUERY_SCALE).astype(bf16)
        for g in range(2):
            qp[g, h * 128 : (h + 1) * 128, :] = normed[g * 128 : (g + 1) * 128]
        for e in range(2):
            low = e * 128 + h * 64
            qa[low : low + 64, :] = normed[256 + e * 64 : 320 + e * 64]

    def scored(queries, keys_):
        return jnp.exp(
            lax.dot_general(
                queries, keys_, (((1,), (1,)), ((), ())), preferred_element_type=f32
            )
        )

    def add_in(slot, weights, values_):
        part = weights[:, :128]
        if weights.shape[1] == 256:
            part = part + weights[:, 128:]
        tot[slot] += part
        num[slot] += jnp.dot(weights.astype(bf16), values_, preferred_element_type=f32)

    num[...] = jnp.zeros_like(num)
    tot[...] = jnp.zeros_like(tot)

    row_ = lax.broadcasted_iota(jnp.int32, (256, 128), 0)
    col_ = lax.broadcasted_iota(jnp.int32, (256, 128), 1)
    own = scored(qa[...], akv[:, :128])
    own_seen = (row_ // 128 == col_ // 64) & (col_ % 64 <= row_ % 64)
    add_in(2, jnp.where(own_seen, own, 0.0), akv[:, 128:])

    row = lax.broadcasted_iota(jnp.int32, (256, 256), 0)
    col = lax.broadcasted_iota(jnp.int32, (256, 256), 1)

    def prompt_step(k):
        zs = (z + 8 - k) % 8
        ahead = c * 128 + 256 * k + row % 128 - col

        def one(g, source):
            pair = kvg[source, zs].reshape(256, 256)
            weights = scored(qp[g], pair[:, :128])
            if k == 0:
                weights = jnp.where(ahead >= 0, weights, 0.0)
            if k == 4:
                weights = jnp.where(ahead < 1024, weights, 0.0)
            add_in(g, weights, pair[:, 128:])

        if k == 0:
            one(0, 0)
            one(1, 1)
        else:

            @pl.when(z >= k)
            def _():
                one(0, 0)

            one(1, (z + 8 - k) // 8)

    def kv_sib(g, zs):
        arrived(kvg.at[g, zs, 1 - c], kv_ss.at[2, g, zs], kv_rs.at[g, zs, 1 - c])

    kv_sib(0, z)
    kv_sib(1, z)
    prompt_step(0)
    for k in range(1, 5):
        zs = (z + 8 - k) % 8
        zn = (z + k) % 8
        for g in range(2):
            arrived(kvg.at[g, zs, c], kv_ss.at[2, g, zs], kv_rs.at[g, zs, c])
            if k < 4:
                kv_send(g, zs, 0, z_fwd)
            kv_send(g, zs, 2, sib)
        if k < 4:
            arrived(kvg.at[1, zn, c], kv_ss.at[2, 1, zn], kv_rs.at[1, zn, c])
            if k < 3:
                kv_send(1, zn, 1, z_bwd)
            kv_send(1, zn, 2, sib)
        if k < 3:
            o_step(k + 2)
        for g in range(2):
            kv_sib(g, zs)
        if k < 4:
            kv_sib(1, zn)
        prompt_step(k)

    for zz in range(4, 8):
        pair = kvg[1, zz].reshape(256, 256)
        weights = scored(qa[...], pair[:, :128])
        if zz == 4:
            weights = jnp.where(col > row % 64, weights, 0.0)
        add_in(2, weights, pair[:, 128:])

    for g in range(2):
        out = num[g] / jnp.sum(tot[g], axis=-1, keepdims=True)
        for h in range(2):
            att[g * 128 : (g + 1) * 128, h * 128 : (h + 1) * 128] = out[
                h * 128 : (h + 1) * 128
            ].astype(bf16)
    out = num[2] / jnp.sum(tot[2], axis=-1, keepdims=True)
    for e in range(2):
        for h in range(2):
            low = e * 128 + h * 64
            att[256 + e * 64 : 320 + e * 64, h * 128 : (h + 1) * 128] = out[
                low : low + 64
            ].astype(bf16)

    for zz in range(8):
        slot = zz * 2 + 1 - c
        arrived(og.at[slot], o_ss.at[2, slot], o_rs.at[slot])

    for q, (start, width, axis) in enumerate(RS):
        cols = slice(start, start + width)
        left = jnp.dot(
            att[...],
            og[:, :, start : start + width].reshape(256, width),
            preferred_element_type=f32,
        )
        right = jnp.dot(
            att[...],
            og[:, :, HALF + start : HALF + start + width].reshape(256, width),
            preferred_element_type=f32,
        )
        for y_ in range(4):
            for x_ in range(4):
                i, j = (x_, y_) if axis == "x" else (y_, x_)
                p = y_ * 4 + x_
                sb[i, j, 0:16, cols] = left[p * 16 : p * 16 + 16].astype(bf16)
                sb[i, j, 16:32, cols] = right[p * 16 : p * 16 + 16].astype(bf16)
                low = 256 + p * 8
                sb[i, j, 32:48, cols] = jnp.concatenate(
                    [left[low : low + 8], right[low : low + 8]], 0
                ).astype(bf16)
        mi = x if axis == "x" else y
        for d in ORDER:
            send(
                sb.at[(mi + d) % 4, :, :, pl.ds(start, width)],
                r1.at[d - 1, :, :, pl.ds(start, width)],
                r1_ss.at[q, d - 1],
                r1_rs.at[q, d - 1],
                peer(axis, d),
            )
    for q, (start, width, axis) in enumerate(RS):
        cols = slice(start, start + width)
        mi, mj = (x, y) if axis == "x" else (y, x)
        for d in ORDER:
            arrived(
                r1.at[d - 1, :, :, pl.ds(start, width)],
                r1_ss.at[q, d - 1],
                r1_rs.at[q, d - 1],
            )
        total = sb[mi, :, :, cols].astype(f32)
        for d in range(3):
            total = total + r1[d, :, :, cols].astype(f32)
        s2[:, :, cols] = total.astype(bf16)
        for d in ORDER:
            send(
                s2.at[(mj + d) % 4, :, pl.ds(start, width)],
                r2.at[d - 1, :, pl.ds(start, width)],
                r2_ss.at[q, d - 1],
                r2_rs.at[q, d - 1],
                peer("y" if axis == "x" else "x", d),
            )
    for q, (start, width, axis) in enumerate(RS):
        cols = slice(start, start + width)
        mj = y if axis == "x" else x
        for d in ORDER:
            arrived(
                r2.at[d - 1, :, pl.ds(start, width)],
                r2_ss.at[q, d - 1],
                r2_rs.at[q, d - 1],
            )
        total = s2[mj, :, cols].astype(f32)
        for d in range(3):
            total = total + r2[d, :, cols].astype(f32)
        mix[:, cols] = total

    def square_sum(part):
        return jnp.sum(part * part, axis=-1, keepdims=True)

    left, right = mix[0:16, :], mix[16:32, :]
    scale = lax.rsqrt((square_sum(left) + square_sum(right)) / D + EPS)
    p_out[:, :HALF] = (
        prompt[:, :HALF].astype(f32) + left * scale * post_gain[:, :HALF]
    ).astype(bf16)
    p_out[:, HALF:] = (
        prompt[:, HALF:].astype(f32) + right * scale * post_gain[:, HALF:]
    ).astype(bf16)
    left, right = mix[32:40, :], mix[40:48, :]
    scale = lax.rsqrt((square_sum(left) + square_sum(right)) / D + EPS)
    position = tp * 8 + lax.broadcasted_iota(jnp.int32, (8, HALF), 0)
    live = position < lens[0]
    a_out[:, :HALF] = jnp.where(
        live, answers[:, :HALF].astype(f32) + left * scale * post_gain[:, :HALF], 0.0
    ).astype(bf16)
    a_out[:, HALF:] = jnp.where(
        live, answers[:, HALF:].astype(f32) + right * scale * post_gain[:, HALF:], 0.0
    ).astype(bf16)

    for copy in started:
        copy.wait_send()


def on_device(
    prompt,
    answers,
    answer_lengths,
    input_gain,
    query_weight,
    key_weight,
    value_weight,
    query_gain,
    key_gain,
    out_weight,
    post_gain,
):
    vmem = pl.BlockSpec(memory_space=pltpu.VMEM)
    dma = pltpu.SemaphoreType.DMA
    n_ag, n_rs = len(AG), len(RS)
    prompt_out, answer_out = pl.pallas_call(
        kernel,
        out_shape=(
            jax.ShapeDtypeStruct((16, D), bf16),
            jax.ShapeDtypeStruct((8, D), bf16),
        ),
        in_specs=[vmem, vmem, pl.BlockSpec(memory_space=pltpu.SMEM)] + [vmem] * 8,
        out_specs=(vmem, vmem),
        scratch_shapes=[
            pltpu.VMEM((2, 2, PAD_W, 256), bf16),
            pltpu.VMEM((3, PAD_W, 256), bf16),
            pltpu.VMEM((2, D, 256), bf16),
            pltpu.VMEM((4, 4, 48, HALF), bf16),
            pltpu.VMEM((384, 256), f32),
            pltpu.VMEM((2, 8, 2, 128, 256), bf16),
            pltpu.VMEM((128, 256), bf16),
            pltpu.VMEM((2, 256, 128), bf16),
            pltpu.VMEM((256, 128), bf16),
            pltpu.VMEM((3, 256, 128), f32),
            pltpu.VMEM((3, 256, 128), f32),
            pltpu.VMEM((384, 256), bf16),
            pltpu.VMEM((16, 16, D), bf16),
            pltpu.VMEM((4, 4, 48, HALF), bf16),
            pltpu.VMEM((3, 4, 48, HALF), bf16),
            pltpu.VMEM((4, 48, HALF), bf16),
            pltpu.VMEM((3, 48, HALF), bf16),
            pltpu.VMEM((48, HALF), f32),
            dma((3,)),
            dma((3,)),
            dma((3, 16)),
            dma((2, 16)),
            dma((3, 16)),
            dma((16,)),
            dma((3, 2, 8)),
            dma((2, 8, 2)),
            dma((n_ag, 2, 3)),
            dma((n_ag, 2, 3)),
            dma((n_rs, 3)),
            dma((n_rs, 3)),
            dma((n_rs, 3)),
            dma((n_rs, 3)),
        ],
        compiler_params=pltpu.CompilerParams(
            collective_id=0, has_side_effects=True, vmem_limit_bytes=56 * 1024 * 1024
        ),
        name="sublayer",
    )(
        prompt,
        answers[0],
        answer_lengths,
        input_gain[None],
        query_weight,
        key_weight,
        value_weight,
        query_gain[None],
        key_gain[None],
        out_weight,
        post_gain[None],
    )
    return prompt_out, answer_out[None]


def solution(mesh):
    placed = (
        P(("seq", "tp"), None),
        P("seq", "tp", None),
        P("seq"),
        P(),
        P("seq", "tp"),
        P("seq", "tp"),
        P("seq", "tp"),
        P(),
        P(),
        P(("tp", "seq"), None),
        P(),
    )
    return jax.shard_map(
        on_device,
        mesh=mesh,
        in_specs=placed,
        out_specs=(P(("seq", "tp"), None), P("seq", "tp", None)),
        check_vma=False,
    )
```

time: 823 us -> 116 us (0.14)
  waiting for transfers between devices: 701 us -> 0 us
  Pallas kernels: 0 us -> 110 us
  starting transfers between devices: 31.7 us -> 0 us
  blocking collectives: 26 us -> 0 us
  matrix products: 17.2 us -> 0 us
  between operations: 15.3 us -> 1.3 us
  local copies, waits for them, and re-layouts: 16.4 us -> 4.26 us
  other arithmetic: 11.1 us -> 0 us
    all_gather x5 -> x0, waiting for transfers between devices: 354 us -> none  [the longest x1 89.6 us: on_device(): lax.all_gather(query_weight, 'seq', axis=0, tiled=True)]
    psum x1 -> x0, waiting for transfers between devices: 261 us -> none  [broadcast(): return lax.psum(block, axis)]
    pallas_call x0 -> x1, Pallas kernels: none -> 110 us  [on_device(): pl.pallas_call(kernel, out_shape=(jax.ShapeDtypeStruct((16, D), bf16), ja...]
    reduce_scatter x2 -> x0, waiting for transfers between devices: 71.6 us -> none  [the longest x1 41.7 us: on_device(): lax.psum_scatter(mixed[:tok_dev][None].astype(jnp.bfloat16), 'tp', scatte...]
    ppermute x8 -> x0, starting transfers between devices: 31.4 us -> none  [passed_along(): return lax.ppermute(value, axis, pairs)]
    all_gather x1 -> x0, blocking collectives: 26 us -> none  [on_device(): lax.all_gather(answers, 'tp', axis=1, tiled=True)]
    dot_general x12 -> x0, matrix products: 17.2 us -> none  [the longest x3 8.9 us: project_in(): return jnp.dot(normed, weight_full, preferred_element_type=jnp.float32)]
    ppermute x8 -> x0, waiting for transfers between devices: 11.3 us -> none  [passed_along(): return lax.ppermute(value, axis, pairs)]
  transfers between devices with their start and end apart: 16 -> 0, of which waited for: 12 -> 0; matrix products, arithmetic and copies ran while one was open for 4% -> 0% of each run, Pallas kernels for 0% -> 0%
where the time goes in v1:
time: 116 us
  Pallas kernels  110 us (95%)
  local copies, waits for them, and re-layouts  4.26 us (4%)
  between operations  1.3 us (1%)
    pallas_call x1, Pallas kernels, on_device(): pl.pallas_call(kernel, out_shape=(jax.ShapeDtypeStruct((16, D), bf16), ja...  110 us

profile of v1, /device:TPU:1, one launch (start us, length us, event | category | flops | bytes accessed | tf_op | source)
XLA Modules:
  0.0 115.7 jit_solution(10517094031154114489)
XLA Ops:
  1.3 0.0 copy-start.1
  1.3 1.4 %broadcast_in_dim.15.in_gain = f32[1,5376]{1,0:T(1,128)} reshape(f32[5376]{0:T(1024)} %param.14) | data formatting | bytes 43008 | tf_op jit(solution)/shard_map/broadcast_in_dim | solution.py:584
  2.7 0.0 copy-done.1
  2.7 0.6 broadcast_in_dim.18.post_gain
  3.3 110.1 %sublayer.1 = (bf16[16,5376]{1,0:T(8,128)(2,1)}, bf16[8,5376]{1,0:T(8,128)(2,1)}) custom-call(bf16[16,5376]{1,0:T(8,128)(2,1)} %prompt.1, bf16[8,5376]{1,0:T(8,128)(2,1)} %bitcast.5, s32[1]{0:T(128)S(6)} %copy.15.lens, f32[1,5376]{1,0:T(1,128)} %broadcast_in_dim.15.in_gain, bf16[168,512]{1,0:T(8,128)(2,1)} %wq.1, bf16[168,256]{1,0:T(8,128)(2,1)} %wk.1, ...), custom_call_target="tpu_custom_call" | custom-call | tf_op jit(solution)/shard_map/sublayer/pallas_call | solution.py:534
  113.4 0.0 copy-start
  113.4 1.6 %copy.16 = bf16[16,5376]{1,0:T(8,128)(2,1)} copy(bf16[16,5376]{1,0:T(8,128)(2,1)} %get-tuple-element.8) | data formatting | bytes 344064
  115.1 0.0 copy-done
  115.1 0.6 copy.17
Async XLA Ops:
  1.3 1.4 %copy-start.1 = (f32[5376]{0:T(1024)S(1)}, f32[5376]{0:T(1024)}, u32[]{:S(2)}) copy-start(f32[5376]{0:T(1024)} %param.21) | copy-start | bytes 64516
  113.4 1.6 %copy-start = (bf16[8,5376]{1,0:T(8,128)(2,1)S(1)}, bf16[8,5376]{1,0:T(8,128)(2,1)}, u32[]{:S(2)}) copy-start(bf16[8,5376]{1,0:T(8,128)(2,1)} %get-tuple-element.5) | copy-start | bytes 258052

commit v2 on v1

v2 whole, which is shorter than its diff:
```python
import jax
import jax.numpy as jnp
from jax import lax
from jax.experimental import pallas as pl
from jax.experimental.pallas import tpu as pltpu
from jax.sharding import PartitionSpec as P

D = 5376
HALF = D // 2
HEAD = 128
ROWS_W = 168
PAIR_W = 2 * ROWS_W
PAD_W = 176
EPS = 1e-06
QUERY_SCALE = 168.0 ** (-0.5)
KC = 896

bf16 = jnp.bfloat16
f32 = jnp.float32

AG = (
    (0, 32, 0, 640, "x"),
    (0, 32, 640, 640, "y"),
    (0, 32, 1280, 640, "x"),
    (0, 32, 1920, 768, "y"),
    (32, 16, 0, 1280, "x"),
    (32, 16, 1280, 1408, "y"),
)
RS = (
    (0, 384, "x"),
    (384, 512, "y"),
    (896, 512, "x"),
    (1408, 384, "y"),
    (1792, 384, "x"),
    (2176, 512, "y"),
)
ORDER = (1, 3, 2)
O_REACH = (2, 5)


def kernel(
    prompt,
    answers,
    lens,
    in_gain,
    wq,
    wk,
    wv,
    q_gain,
    k_gain,
    wo,
    post_gain,
    p_out,
    a_out,
    st,
    rx,
    wg,
    xg,
    acc,
    kvg,
    akv,
    qp,
    qa,
    num,
    tot,
    att,
    og,
    sb,
    ra,
    r1,
    s2,
    r2,
    mix,
    e_ss,
    e_rs,
    w_ss,
    w_rs,
    o_ss,
    o_rs,
    kv_ss,
    kv_rs,
    ag_ss,
    ag_rs,
    rs_ss,
    rs_rs,
):
    seq = lax.axis_index("seq")
    tp = lax.axis_index("tp")
    yh, z, c = seq // 16, (seq // 2) % 8, seq % 2
    yl, x = tp // 4, tp % 4
    y = yh * 2 + yl

    def dev(y_, x_, z_, c_):
        return ((y_ // 2) * 16 + z_ * 2 + c_, (y_ % 2) * 4 + x_)

    sib = dev(y, x, z, 1 - c)
    z_to = (dev(y, x, (z + 1) % 8, c), dev(y, x, (z + 7) % 8, c))
    diag = dev((y + 2) % 4, x, z, 1 - c)

    def peer(axis, d):
        if axis == "x":
            return dev(y, (x + d) % 4, z, c)
        return dev((y + d) % 4, x, z, c)

    partners = [sib, *z_to, diag] + [peer(a, d) for a in "xy" for d in ORDER]
    barrier = pltpu.get_barrier_semaphore()
    for target in partners:
        pl.semaphore_signal(
            barrier, inc=1, device_id=target, device_id_type=pl.DeviceIdType.MESH
        )

    started = []

    def send(src, dst, send_sem, recv_sem, target):
        copy = pltpu.make_async_remote_copy(
            src_ref=src,
            dst_ref=dst,
            send_sem=send_sem,
            recv_sem=recv_sem,
            device_id=target,
            device_id_type=pl.DeviceIdType.MESH,
        )
        copy.start()
        started.append(copy)

    def arrived(dst, recv_sem):
        pltpu.make_async_remote_copy(
            src_ref=dst,
            dst_ref=dst,
            send_sem=e_ss.at[0, 0],
            recv_sem=recv_sem,
            device_id=sib,
            device_id_type=pl.DeviceIdType.MESH,
        ).wait_recv()

    for h in range(2):
        st[h, 0, 0, :ROWS_W, :] = wk[:, 128 * h : 128 * h + 128]
        st[h, 0, 1, :ROWS_W, :] = wv[:, 128 * h : 128 * h + 128]
        for i in range(2):
            low = 256 * h + 128 * i
            st[h, 1, i, :ROWS_W, :] = wq[:, low : low + 128]
    pl.semaphore_wait(barrier, len(partners))
    for f in range(2):
        send(st.at[yh, f, 1 - c], rx.at[f, 0], e_ss.at[f, 0], e_rs.at[f, 0], sib)
        send(
            st.at[1 - yh, f, c], rx.at[f, 1], e_ss.at[f, 1], e_rs.at[f, 1], peer("y", 2)
        )
        send(st.at[1 - yh, f, 1 - c], rx.at[f, 2], e_ss.at[f, 2], e_rs.at[f, 2], diag)

    def ag_one(q, y_, x_):
        row, count, start, width, _ = AG[q]
        return xg.at[y_, x_, pl.ds(row, count), pl.ds(start, width)]

    def ag_line(q, k):
        row, count, start, width, axis = AG[q]
        rows_, cols_ = pl.ds(row, count), pl.ds(start, width)
        if axis == "x":
            return xg.at[k, :, rows_, cols_]
        return xg.at[:, k, rows_, cols_]

    def ag_axes(q):
        if AG[q][4] == "x":
            return "x", "y", x, y
        return "y", "x", y, x

    def ag_a(q):
        first, _, _, _ = ag_axes(q)
        mine = ag_one(q, y, x)
        for d in ORDER:
            send(mine, mine, ag_ss.at[q, d - 1], ag_rs.at[q, d - 1], peer(first, d))

    def ag_b(q):
        first, second, _, own = ag_axes(q)
        for d in ORDER:
            if first == "x":
                piece = ag_one(q, y, (x + 4 - d) % 4)
            else:
                piece = ag_one(q, (y + 4 - d) % 4, x)
            arrived(piece, ag_rs.at[q, d - 1])
        mine = ag_line(q, own)
        for d in ORDER:
            send(mine, mine, ag_ss.at[q, 2 + d], ag_rs.at[q, 2 + d], peer(second, d))

    def ag_done(q):
        _, _, _, own = ag_axes(q)
        for d in ORDER:
            arrived(ag_line(q, (own + 4 - d) % 4), ag_rs.at[q, 2 + d])

    def w_block(f, core, m):
        return wg.at[2 * f + core, pl.ds(pl.multiple_of(m * PAIR_W, 16), PAIR_W), :]

    def w_index(h, dz):
        return ((yh + h) % 2) * 8 + (z + dz) % 8

    def w_send(f, m, way):
        piece = w_block(f, c, m)
        target = sib if way == 2 else z_to[way]
        send(piece, piece, w_ss.at[f, way, m], w_rs.at[f, c, m], target)

    def w_own(f, h):
        if h == 0:
            arrived(rx.at[f, 0], e_rs.at[f, 0])
            mine = st[yh, f, c, :ROWS_W, :].astype(f32)
            other = rx[f, 0, :ROWS_W, :].astype(f32)
        else:
            arrived(rx.at[f, 1], e_rs.at[f, 1])
            arrived(rx.at[f, 2], e_rs.at[f, 2])
            mine = rx[f, 1, :ROWS_W, :].astype(f32)
            other = rx[f, 2, :ROWS_W, :].astype(f32)
        low = jnp.where(c == 0, mine, other)
        high = jnp.where(c == 0, other, mine)
        m = w_index(h, 0)
        wg[2 * f + c, pl.ds(pl.multiple_of(m * PAIR_W, 16), PAIR_W), :] = (
            jnp.concatenate([low, high], 0).astype(bf16)
        )
        for way in range(3):
            w_send(f, m, way)

    def w_step(f, k):
        for h in range(2):
            for way in range(2):
                reach = 4 if h == way else 3
                if k <= reach:
                    m = w_index(h, 8 - k if way == 0 else k)
                    arrived(w_block(f, c, m), w_rs.at[f, c, m])
                    if k < reach:
                        w_send(f, m, way)
                    w_send(f, m, 2)

    def w_done(f):
        for m in range(16):
            arrived(w_block(f, 1 - c, m), w_rs.at[f, 1 - c, m])

    def o_send(slot, way):
        piece = og.at[slot]
        target = sib if way == 2 else z_to[way]
        send(piece, piece, o_ss.at[way, slot], o_rs.at[slot], target)

    def o_start(*ways):
        for way in ways:
            o_send(z * 2 + c, way)

    def o_step(way, k):
        slot = ((z + (8 - k if way == 0 else k)) % 8) * 2 + c
        arrived(og.at[slot], o_rs.at[slot])
        if k < O_REACH[way]:
            o_send(slot, way)
        o_send(slot, 2)

    def o_done():
        for zz in range(8):
            slot = zz * 2 + 1 - c
            arrived(og.at[slot], o_rs.at[slot])

    def drain():
        while started:
            started.pop(0).wait_send()

    def kv_send(g, zs, way):
        piece = kvg.at[g, zs, c]
        target = sib if way == 2 else z_to[way]
        send(piece, piece, kv_ss.at[way, g, zs], kv_rs.at[g, zs, c], target)

    def kv_start():
        for g in range(2):
            kv_send(g, z, 0)
        kv_send(1, z, 1)
        for g in range(2):
            kv_send(g, z, 2)

    def kv_step(k):
        zs = (z + 8 - k) % 8
        zn = (z + k) % 8
        for g in range(2):
            arrived(kvg.at[g, zs, c], kv_rs.at[g, zs, c])
            if k < 4:
                kv_send(g, zs, 0)
            kv_send(g, zs, 2)
        if k < 4:
            arrived(kvg.at[1, zn, c], kv_rs.at[1, zn, c])
            if k < 3:
                kv_send(1, zn, 1)
            kv_send(1, zn, 2)

    def kv_done(k):
        zs = (z + 8 - k) % 8
        zn = (z + k) % 8
        for g in range(2):
            arrived(kvg.at[g, zs, 1 - c], kv_rs.at[g, zs, 1 - c])
        if 0 < k < 4:
            arrived(kvg.at[1, zn, 1 - c], kv_rs.at[1, zn, 1 - c])

    def project(f):
        acc[0:256, 256 * f : 256 * f + 256] = jnp.zeros((256, 256), f32)
        for h in range(2):

            def body(i, carry):
                cols_ = pl.ds(pl.multiple_of(i * KC, 128), KC)
                krows = pl.ds(pl.multiple_of(h * HALF + i * KC, 128), KC)
                acc[0:256, 256 * f : 256 * f + 256] += jnp.dot(
                    xg[:, :, 16 * h : 16 * h + 16, cols_].reshape(256, KC),
                    jnp.concatenate([wg[2 * f, krows, :], wg[2 * f + 1, krows, :]], 1),
                    preferred_element_type=f32,
                )
                return carry

            lax.fori_loop(0, HALF // KC, body, 0)

    def project_answers():
        acc[256:384, :] = jnp.zeros((128, 512), f32)
        for h in range(2):

            def body(i, carry):
                cols_ = pl.ds(pl.multiple_of(i * KC, 128), KC)
                krows = pl.ds(pl.multiple_of(h * HALF + i * KC, 128), KC)
                tail = xg[:, :, 32:48, cols_].astype(f32)
                tail = tail[:, :, 8 * h : 8 * h + 8, :].reshape(128, KC).astype(bf16)
                acc[256:384, :] += jnp.dot(
                    tail,
                    jnp.concatenate([wg[i_, krows, :] for i_ in range(4)], 1),
                    preferred_element_type=f32,
                )
                return carry

            lax.fori_loop(0, HALF // KC, body, 0)

    def head_norm(raw, gains):
        return raw * lax.rsqrt(jnp.mean(raw * raw, axis=-1, keepdims=True) + EPS) * gains

    def scored(queries, keys_):
        return jnp.exp(
            lax.dot_general(
                queries, keys_, (((1,), (1,)), ((), ())), preferred_element_type=f32
            )
        )

    def add_in(slot, weights, values_):
        part = weights[:, :128]
        if weights.shape[1] == 256:
            part = part + weights[:, 128:]
        tot[slot] += part
        num[slot] += jnp.dot(weights.astype(bf16), values_, preferred_element_type=f32)

    row = lax.broadcasted_iota(jnp.int32, (256, 256), 0)
    col = lax.broadcasted_iota(jnp.int32, (256, 256), 1)

    def prompt_step(k):
        zs = (z + 8 - k) % 8
        ahead = c * 128 + 256 * k + row % 128 - col

        def one(g, source):
            pair = kvg[source, zs].reshape(256, 256)
            weights = scored(qp[g], pair[:, :128])
            if k == 0:
                weights = jnp.where(ahead >= 0, weights, 0.0)
            if k == 4:
                weights = jnp.where(ahead < 1024, weights, 0.0)
            add_in(g, weights, pair[:, 128:])

        if k == 0:
            one(0, 0)
            one(1, 1)
        else:

            @pl.when(z >= k)
            def _():
                one(0, 0)

            one(1, (z + 8 - k) // 8)

    og[z * 2 + c] = wo[...]
    o_start(0, 1, 2)
    gain = in_gain[...].reshape(1, D)
    rows = prompt[...].astype(f32)
    rows = rows * lax.rsqrt(jnp.mean(rows * rows, axis=-1, keepdims=True) + EPS) * gain
    xg[y, x, 0:16, :] = rows[:, :HALF].astype(bf16)
    xg[y, x, 16:32, :] = rows[:, HALF:].astype(bf16)
    for q in range(4):
        ag_a(q)
    w_own(0, 0)
    rows = answers[...].astype(f32)
    rows = rows * lax.rsqrt(jnp.mean(rows * rows, axis=-1, keepdims=True) + EPS) * gain
    xg[y, x, 32:48, :] = jnp.concatenate([rows[:, :HALF], rows[:, HALF:]], 0).astype(bf16)
    ag_a(4)
    ag_a(5)
    w_own(0, 1)
    for q in range(4):
        ag_b(q)
    w_step(0, 1)
    w_own(1, 0)
    w_own(1, 1)
    w_step(0, 2)
    w_step(1, 1)
    w_step(0, 3)
    o_step(0, 1)
    o_step(1, 1)
    ag_b(4)
    ag_b(5)
    w_step(1, 2)
    w_step(0, 4)
    for q in range(4):
        ag_done(q)
    w_done(0)
    project(0)
    keys = head_norm(acc[0:256, :128], k_gain[...]).astype(bf16)
    values = acc[0:256, 128:256].astype(bf16)
    for g in range(2):
        kvg[g, z, c, :, :128] = keys[g * 128 : (g + 1) * 128]
        kvg[g, z, c, :, 128:] = values[g * 128 : (g + 1) * 128]
    kv_start()
    w_step(1, 3)
    o_step(1, 2)
    kv_step(1)
    w_step(1, 4)
    o_step(1, 3)
    o_step(0, 2)
    w_done(1)
    project(1)
    for h in range(2):
        raw = acc[0:256, 256 + 128 * h : 384 + 128 * h]
        normed = (head_norm(raw, q_gain[...]) * QUERY_SCALE).astype(bf16)
        for g in range(2):
            qp[g, h * 128 : (h + 1) * 128, :] = normed[g * 128 : (g + 1) * 128]
    kv_step(2)
    o_step(1, 4)
    num[...] = jnp.zeros_like(num)
    tot[...] = jnp.zeros_like(tot)
    kv_done(0)
    prompt_step(0)
    kv_done(1)
    prompt_step(1)
    for q in (4, 5):
        ag_done(q)
    project_answers()
    kv_step(3)
    keys = head_norm(acc[256:384, :128], k_gain[...]).astype(bf16)
    akv[:, :128] = keys
    akv[:, 128:] = acc[256:384, 128:256].astype(bf16)
    for h in range(2):
        raw = acc[256:384, 256 + 128 * h : 384 + 128 * h]
        normed = (head_norm(raw, q_gain[...]) * QUERY_SCALE).astype(bf16)
        for e in range(2):
            low = e * 128 + h * 64
            qa[low : low + 64, :] = normed[e * 64 : e * 64 + 64]
    kv_done(2)
    prompt_step(2)
    kv_step(4)
    row_ = lax.broadcasted_iota(jnp.int32, (256, 128), 0)
    col_ = lax.broadcasted_iota(jnp.int32, (256, 128), 1)
    own = scored(qa[...], akv[:, :128])
    own_seen = (row_ // 128 == col_ // 64) & (col_ % 64 <= row_ % 64)
    add_in(2, jnp.where(own_seen, own, 0.0), akv[:, 128:])
    kv_done(3)
    prompt_step(3)
    kv_done(4)
    prompt_step(4)
    for zz in range(4, 8):
        pair = kvg[1, zz].reshape(256, 256)
        weights = scored(qa[...], pair[:, :128])
        if zz == 4:
            weights = jnp.where(col > row % 64, weights, 0.0)
        add_in(2, weights, pair[:, 128:])


    o_step(1, 5)

    for g in range(2):
        out = num[g] / jnp.sum(tot[g], axis=-1, keepdims=True)
        for h in range(2):
            att[g * 128 : (g + 1) * 128, h * 128 : (h + 1) * 128] = out[
                h * 128 : (h + 1) * 128
            ].astype(bf16)
    out = num[2] / jnp.sum(tot[2], axis=-1, keepdims=True)
    for e in range(2):
        for h in range(2):
            low = e * 128 + h * 64
            att[256 + e * 64 : 320 + e * 64, h * 128 : (h + 1) * 128] = out[
                low : low + 64
            ].astype(bf16)

    def rs_axes(q):
        if RS[q][2] == "x":
            return "x", "y", x, y
        return "y", "x", y, x

    def rs_a(q):
        start, width, axis = RS[q]
        cols_ = slice(start, start + width)
        left = jnp.dot(
            att[...],
            og[:, :, start : start + width].reshape(256, width),
            preferred_element_type=f32,
        )
        right = jnp.dot(
            att[...],
            og[:, :, HALF + start : HALF + start + width].reshape(256, width),
            preferred_element_type=f32,
        )
        for y_ in range(4):
            for x_ in range(4):
                i, k = (x_, y_) if axis == "x" else (y_, x_)
                p = y_ * 4 + x_
                sb[i, k, 0:16, cols_] = left[p * 16 : p * 16 + 16].astype(bf16)
                sb[i, k, 16:32, cols_] = right[p * 16 : p * 16 + 16].astype(bf16)
                low_ = 256 + p * 8
                sb[i, k, 32:48, cols_] = jnp.concatenate(
                    [left[low_ : low_ + 8], right[low_ : low_ + 8]], 0
                ).astype(bf16)
        first, _, mi, _ = rs_axes(q)
        cols_ = pl.ds(start, width)
        for w, d in enumerate((1, 3)):
            send(
                sb.at[(mi + 2) % 4, pl.ds(2 * w, 2), :, cols_],
                ra.at[w, :, :, cols_],
                rs_ss.at[q, w],
                rs_rs.at[q, w],
                peer(first, d),
            )

    def rs_b(q):
        start, width, _ = RS[q]
        first, _, mi, _ = rs_axes(q)
        cols_ = slice(start, start + width)
        for w, d in enumerate((1, 3)):
            arrived(ra.at[w, :, :, pl.ds(start, width)], rs_rs.at[q, w])
            i = (mi + d) % 4
            sb[i, 2 * w : 2 * w + 2, :, cols_] = (
                sb[i, 2 * w : 2 * w + 2, :, cols_].astype(f32)
                + ra[w, :, :, cols_].astype(f32)
            ).astype(bf16)
            send(
                sb.at[i, :, :, pl.ds(start, width)],
                r1.at[w, :, :, pl.ds(start, width)],
                rs_ss.at[q, 2 + w],
                rs_rs.at[q, 2 + w],
                peer(first, d),
            )

    def rs_c(q):
        start, width, _ = RS[q]
        _, second, mi, mj = rs_axes(q)
        cols_ = slice(start, start + width)
        for w in range(2):
            arrived(r1.at[w, :, :, pl.ds(start, width)], rs_rs.at[q, 2 + w])
        s2[:, :, cols_] = (
            sb[mi, :, :, cols_].astype(f32)
            + r1[0, :, :, cols_].astype(f32)
            + r1[1, :, :, cols_].astype(f32)
        ).astype(bf16)
        for d in ORDER:
            send(
                s2.at[(mj + d) % 4, :, pl.ds(start, width)],
                r2.at[d - 1, :, pl.ds(start, width)],
                rs_ss.at[q, 3 + d],
                rs_rs.at[q, 3 + d],
                peer(second, d),
            )

    def rs_d(q):
        start, width, _ = RS[q]
        _, _, _, mj = rs_axes(q)
        cols_ = slice(start, start + width)
        for d in ORDER:
            arrived(r2.at[d - 1, :, pl.ds(start, width)], rs_rs.at[q, 3 + d])
        total = s2[mj, :, cols_].astype(f32)
        for d in range(3):
            total = total + r2[d, :, cols_].astype(f32)
        mix[:, cols_] = total

    o_done()
    for q in range(len(RS)):
        rs_a(q)
    drain()
    for q in range(len(RS)):
        rs_b(q)
    for q in range(len(RS)):
        rs_c(q)
    for q in range(len(RS)):
        rs_d(q)

    gain = post_gain[...].reshape(1, D)

    def square_sum(part):
        return jnp.sum(part * part, axis=-1, keepdims=True)

    left, right = mix[0:16, :], mix[16:32, :]
    scale = lax.rsqrt((square_sum(left) + square_sum(right)) / D + EPS)
    p_out[:, :HALF] = (
        prompt[:, :HALF].astype(f32) + left * scale * gain[:, :HALF]
    ).astype(bf16)
    p_out[:, HALF:] = (
        prompt[:, HALF:].astype(f32) + right * scale * gain[:, HALF:]
    ).astype(bf16)
    left, right = mix[32:40, :], mix[40:48, :]
    scale = lax.rsqrt((square_sum(left) + square_sum(right)) / D + EPS)
    position = tp * 8 + lax.broadcasted_iota(jnp.int32, (8, HALF), 0)
    live = position < lens[0]
    a_out[:, :HALF] = jnp.where(
        live, answers[:, :HALF].astype(f32) + left * scale * gain[:, :HALF], 0.0
    ).astype(bf16)
    a_out[:, HALF:] = jnp.where(
        live, answers[:, HALF:].astype(f32) + right * scale * gain[:, HALF:], 0.0
    ).astype(bf16)

    drain()


def on_device(
    prompt,
    answers,
    answer_lengths,
    input_gain,
    query_weight,
    key_weight,
    value_weight,
    query_gain,
    key_gain,
    out_weight,
    post_gain,
):
    vmem = pl.BlockSpec(memory_space=pltpu.VMEM)
    dma = pltpu.SemaphoreType.DMA
    n_ag, n_rs = len(AG), len(RS)
    prompt_out, answer_out = pl.pallas_call(
        kernel,
        out_shape=(
            jax.ShapeDtypeStruct((16, D), bf16),
            jax.ShapeDtypeStruct((8, D), bf16),
        ),
        in_specs=[vmem, vmem, pl.BlockSpec(memory_space=pltpu.SMEM)] + [vmem] * 8,
        out_specs=(vmem, vmem),
        scratch_shapes=[
            pltpu.VMEM((2, 2, 2, PAD_W, 128), bf16),
            pltpu.VMEM((2, 3, PAD_W, 128), bf16),
            pltpu.VMEM((4, D, 128), bf16),
            pltpu.VMEM((4, 4, 48, HALF), bf16),
            pltpu.VMEM((384, 512), f32),
            pltpu.VMEM((2, 8, 2, 128, 256), bf16),
            pltpu.VMEM((128, 256), bf16),
            pltpu.VMEM((2, 256, 128), bf16),
            pltpu.VMEM((256, 128), bf16),
            pltpu.VMEM((3, 256, 128), f32),
            pltpu.VMEM((3, 256, 128), f32),
            pltpu.VMEM((384, 256), bf16),
            pltpu.VMEM((16, 16, D), bf16),
            pltpu.VMEM((4, 4, 48, HALF), bf16),
            pltpu.VMEM((2, 2, 48, HALF), bf16),
            pltpu.VMEM((2, 4, 48, HALF), bf16),
            pltpu.VMEM((4, 48, HALF), bf16),
            pltpu.VMEM((3, 48, HALF), bf16),
            pltpu.VMEM((48, HALF), f32),
            dma((2, 3)),
            dma((2, 3)),
            dma((2, 3, 16)),
            dma((2, 2, 16)),
            dma((3, 16)),
            dma((16,)),
            dma((3, 2, 8)),
            dma((2, 8, 2)),
            dma((n_ag, 7)),
            dma((n_ag, 7)),
            dma((n_rs, 7)),
            dma((n_rs, 7)),
        ],
        compiler_params=pltpu.CompilerParams(
            collective_id=0, has_side_effects=True, vmem_limit_bytes=56 * 1024 * 1024
        ),
        name="sublayer",
    )(
        prompt,
        answers[0],
        answer_lengths,
        input_gain,
        query_weight,
        key_weight,
        value_weight,
        query_gain[None],
        key_gain[None],
        out_weight,
        post_gain,
    )
    return prompt_out, answer_out[None]


def solution(mesh):
    placed = (
        P(("seq", "tp"), None),
        P("seq", "tp", None),
        P("seq"),
        P(),
        P("seq", "tp"),
        P("seq", "tp"),
        P("seq", "tp"),
        P(),
        P(),
        P(("tp", "seq"), None),
        P(),
    )
    return jax.shard_map(
        on_device,
        mesh=mesh,
        in_specs=placed,
        out_specs=(P(("seq", "tp"), None), P("seq", "tp", None)),
        check_vma=False,
    )
```

time: 116 us -> 105 us (0.905)
  Pallas kernels: 110 us -> 100 us
  local copies, waits for them, and re-layouts: 4.26 us -> 2.27 us
    pallas_call x1, Pallas kernels: 110 us -> 100 us  [on_device(): pl.pallas_call(kernel, out_shape=(jax.ShapeDtypeStruct((16, D), bf16), ja...]
    broadcast_in_dim x2 -> x0, local copies, waits for them, and re-layouts: 1.99 us -> none  [the longest x1 1.36 us: on_device(): input_gain[None]]
where the time goes in v2:
time: 105 us; the launch traced here: 104 us
  Pallas kernels  100 us (95%)
  local copies, waits for them, and re-layouts  2.27 us (2%)
  between operations  1.3 us (1%)
    pallas_call x1, Pallas kernels, on_device(): pl.pallas_call(kernel, out_shape=(jax.ShapeDtypeStruct((16, D), bf16), ja...  100 us
    unnamed x4, local copies, waits for them, and re-layouts  2.27 us

profile of v2, /device:TPU:1, one launch (start us, length us, event | category | flops | bytes accessed | tf_op | source)
XLA Modules:
  0.0 104.0 jit_solution(17147913289178890180)
XLA Ops:
  1.3 100.5 %sublayer.1 = (bf16[16,5376]{1,0:T(8,128)(2,1)}, bf16[8,5376]{1,0:T(8,128)(2,1)}) custom-call(bf16[16,5376]{1,0:T(8,128)(2,1)} %prompt.1, bf16[8,5376]{1,0:T(8,128)(2,1)} %bitcast.5, s32[1]{0:T(128)S(6)} %copy.15.lens, f32[5376]{0:T(1024)} %in_gain.1, bf16[168,512]{1,0:T(8,128)(2,1)} %wq.1, bf16[168,256]{1,0:T(8,128)(2,1)} %wk.1, bf16[168,256]{1,0:T(8,128)(2,1)} %wv.1, ...), custom_call_target="tpu_custom_call" | custom-call | tf_op jit(solution)/shard_map/sublayer/pallas_call | solution.py:624
  101.7 0.0 copy-start
  101.7 1.6 %copy.16 = bf16[16,5376]{1,0:T(8,128)(2,1)} copy(bf16[16,5376]{1,0:T(8,128)(2,1)} %get-tuple-element.8) | data formatting | bytes 344064
  103.4 0.0 copy-done
  103.4 0.6 copy.17
Async XLA Ops:
  101.7 1.6 %copy-start = (bf16[8,5376]{1,0:T(8,128)(2,1)S(1)}, bf16[8,5376]{1,0:T(8,128)(2,1)}, u32[]{:S(2)}) copy-start(bf16[8,5376]{1,0:T(8,128)(2,1)} %get-tuple-element.5) | copy-start | bytes 258052

commit v3 on v2

--- a/solution.py
+++ b/solution.py
@@ -19,23 +19,14 @@
 f32 = jnp.float32
 
 AG = (
-    (0, 32, 0, 640, "x"),
-    (0, 32, 640, 640, "y"),
-    (0, 32, 1280, 640, "x"),
-    (0, 32, 1920, 768, "y"),
+    (0, 32, 0, 1280, "x"),
+    (0, 32, 1280, 1408, "y"),
     (32, 16, 0, 1280, "x"),
     (32, 16, 1280, 1408, "y"),
 )
-RS = (
-    (0, 384, "x"),
-    (384, 512, "y"),
-    (896, 512, "x"),
-    (1408, 384, "y"),
-    (1792, 384, "x"),
-    (2176, 512, "y"),
-)
+RS = ((0, 640, "x"), (640, 640, "y"), (1280, 640, "x"), (1920, 768, "y"))
 ORDER = (1, 3, 2)
-O_REACH = (2, 5)
+O_REACH = (3, 4)
 
 
 def kernel(
@@ -139,8 +130,16 @@
         for i in range(2):
             low = 256 * h + 128 * i
             st[h, 1, i, :ROWS_W, :] = wq[:, low : low + 128]
+    gain = in_gain[...].reshape(1, D)
+    rows = prompt[...].astype(f32)
+    rows = rows * lax.rsqrt(jnp.mean(rows * rows, axis=-1, keepdims=True) + EPS) * gain
+    xg[y, x, 0:16, :] = rows[:, :HALF].astype(bf16)
+    xg[y, x, 16:32, :] = rows[:, HALF:].astype(bf16)
+    rows = answers[...].astype(f32)
+    rows = rows * lax.rsqrt(jnp.mean(rows * rows, axis=-1, keepdims=True) + EPS) * gain
+    xg[y, x, 32:48, :] = jnp.concatenate([rows[:, :HALF], rows[:, HALF:]], 0).astype(bf16)
     pl.semaphore_wait(barrier, len(partners))
-    for f in range(2):
+    def exchange(f):
         send(st.at[yh, f, 1 - c], rx.at[f, 0], e_ss.at[f, 0], e_rs.at[f, 0], sib)
         send(
             st.at[1 - yh, f, c], rx.at[f, 1], e_ss.at[f, 1], e_rs.at[f, 1], peer("y", 2)
@@ -272,15 +271,15 @@
         zs = (z + 8 - k) % 8
         zn = (z + k) % 8
         for g in range(2):
-            arrived(kvg.at[g, zs, c], kv_rs.at[g, zs, c])
-            if k < 4:
-                kv_send(g, zs, 0)
-            kv_send(g, zs, 2)
+            if k < 4 or g == 0:
+                arrived(kvg.at[g, zs, c], kv_rs.at[g, zs, c])
+                if k < 4 - g:
+                    kv_send(g, zs, 0)
+                kv_send(g, zs, 2)
+        arrived(kvg.at[1, zn, c], kv_rs.at[1, zn, c])
         if k < 4:
-            arrived(kvg.at[1, zn, c], kv_rs.at[1, zn, c])
-            if k < 3:
-                kv_send(1, zn, 1)
-            kv_send(1, zn, 2)
+            kv_send(1, zn, 1)
+        kv_send(1, zn, 2)
 
     def kv_done(k):
         zs = (z + 8 - k) % 8
@@ -368,37 +367,33 @@
 
             one(1, (z + 8 - k) // 8)
 
+    exchange(0)
     og[z * 2 + c] = wo[...]
     o_start(0, 1, 2)
-    gain = in_gain[...].reshape(1, D)
-    rows = prompt[...].astype(f32)
-    rows = rows * lax.rsqrt(jnp.mean(rows * rows, axis=-1, keepdims=True) + EPS) * gain
-    xg[y, x, 0:16, :] = rows[:, :HALF].astype(bf16)
-    xg[y, x, 16:32, :] = rows[:, HALF:].astype(bf16)
-    for q in range(4):
+    for q in range(2):
         ag_a(q)
+    exchange(1)
     w_own(0, 0)
-    rows = answers[...].astype(f32)
-    rows = rows * lax.rsqrt(jnp.mean(rows * rows, axis=-1, keepdims=True) + EPS) * gain
-    xg[y, x, 32:48, :] = jnp.concatenate([rows[:, :HALF], rows[:, HALF:]], 0).astype(bf16)
-    ag_a(4)
-    ag_a(5)
+    ag_a(2)
+    ag_a(3)
     w_own(0, 1)
-    for q in range(4):
+    for q in range(2):
         ag_b(q)
     w_step(0, 1)
     w_own(1, 0)
     w_own(1, 1)
     w_step(0, 2)
+    o_step(0, 1)
+    o_step(1, 1)
     w_step(1, 1)
     w_step(0, 3)
-    o_step(0, 1)
-    o_step(1, 1)
-    ag_b(4)
-    ag_b(5)
+    ag_b(2)
+    ag_b(3)
     w_step(1, 2)
     w_step(0, 4)
-    for q in range(4):
+    o_step(1, 2)
+    o_step(0, 2)
+    for q in range(2):
         ag_done(q)
     w_done(0)
     project(0)
@@ -409,11 +404,11 @@
         kvg[g, z, c, :, 128:] = values[g * 128 : (g + 1) * 128]
     kv_start()
     w_step(1, 3)
-    o_step(1, 2)
+    o_step(1, 3)
     kv_step(1)
     w_step(1, 4)
-    o_step(1, 3)
-    o_step(0, 2)
+    o_step(0, 3)
+    kv_step(2)
     w_done(1)
     project(1)
     for h in range(2):
@@ -421,7 +416,7 @@
         normed = (head_norm(raw, q_gain[...]) * QUERY_SCALE).astype(bf16)
         for g in range(2):
             qp[g, h * 128 : (h + 1) * 128, :] = normed[g * 128 : (g + 1) * 128]
-    kv_step(2)
+    kv_step(3)
     o_step(1, 4)
     num[...] = jnp.zeros_like(num)
     tot[...] = jnp.zeros_like(tot)
@@ -429,10 +424,9 @@
     prompt_step(0)
     kv_done(1)
     prompt_step(1)
-    for q in (4, 5):
+    for q in (2, 3):
         ag_done(q)
     project_answers()
-    kv_step(3)
     keys = head_norm(acc[256:384, :128], k_gain[...]).astype(bf16)
     akv[:, :128] = keys
     akv[:, 128:] = acc[256:384, 128:256].astype(bf16)
@@ -461,8 +455,6 @@
             weights = jnp.where(col > row % 64, weights, 0.0)
         add_in(2, weights, pair[:, 128:])
 
-
-    o_step(1, 5)
 
     for g in range(2):
         out = num[g] / jnp.sum(tot[g], axis=-1, keepdims=True)

time: 105 us -> 100 us (0.952)
  Pallas kernels: 100 us -> 96.4 us
    pallas_call x1, Pallas kernels: 100 us -> 96.4 us  [on_device(): pl.pallas_call(kernel, out_shape=(jax.ShapeDtypeStruct((16, D), bf16), ja...]
where the time goes in v3:
time: 100 us
  Pallas kernels  96.4 us (96%)
  local copies, waits for them, and re-layouts  2.27 us (2%)
  between operations  1.3 us (1%)
    pallas_call x1, Pallas kernels, on_device(): pl.pallas_call(kernel, out_shape=(jax.ShapeDtypeStruct((16, D), bf16), ja...  96.4 us
    unnamed x4, local copies, waits for them, and re-layouts  2.27 us

profile of v3, /device:TPU:1, one launch (start us, length us, event | category | flops | bytes accessed | tf_op | source)
XLA Modules:
  0.0 100.0 jit_solution(16321940748309498618)
XLA Ops:
  1.3 96.4 %sublayer.1 = (bf16[16,5376]{1,0:T(8,128)(2,1)}, bf16[8,5376]{1,0:T(8,128)(2,1)}) custom-call(bf16[16,5376]{1,0:T(8,128)(2,1)} %prompt.1, bf16[8,5376]{1,0:T(8,128)(2,1)} %bitcast.5, s32[1]{0:T(128)S(6)} %copy.15.lens, f32[5376]{0:T(1024)} %in_gain.1, bf16[168,512]{1,0:T(8,128)(2,1)} %wq.1, bf16[168,256]{1,0:T(8,128)(2,1)} %wk.1, bf16[168,256]{1,0:T(8,128)(2,1)} %wv.1, ...), custom_call_target="tpu_custom_call" | custom-call | tf_op jit(solution)/shard_map/sublayer/pallas_call | solution.py:616
  97.7 0.0 copy-start
  97.7 1.6 %copy.16 = bf16[16,5376]{1,0:T(8,128)(2,1)} copy(bf16[16,5376]{1,0:T(8,128)(2,1)} %get-tuple-element.8) | data formatting | bytes 344064
  99.4 0.0 copy-done
  99.4 0.6 copy.17
Async XLA Ops:
  97.7 1.6 %copy-start = (bf16[8,5376]{1,0:T(8,128)(2,1)S(1)}, bf16[8,5376]{1,0:T(8,128)(2,1)}, u32[]{:S(2)}) copy-start(bf16[8,5376]{1,0:T(8,128)(2,1)} %get-tuple-element.5) | copy-start | bytes 258052

commit v4 on v3

--- a/solution.py
+++ b/solution.py
@@ -438,7 +438,6 @@
             qa[low : low + 64, :] = normed[e * 64 : e * 64 + 64]
     kv_done(2)
     prompt_step(2)
-    kv_step(4)
     row_ = lax.broadcasted_iota(jnp.int32, (256, 128), 0)
     col_ = lax.broadcasted_iota(jnp.int32, (256, 128), 1)
     own = scored(qa[...], akv[:, :128])
@@ -446,6 +445,7 @@
     add_in(2, jnp.where(own_seen, own, 0.0), akv[:, 128:])
     kv_done(3)
     prompt_step(3)
+    kv_step(4)
     kv_done(4)
     prompt_step(4)
     for zz in range(4, 8):

time: 100 us -> 101 us (1.010)
  no operation moved by 1% of the time
where the time goes in v4:
time: 101 us; the launch traced here: 100 us
  Pallas kernels  96.8 us (96%)
  local copies, waits for them, and re-layouts  2.27 us (2%)
  between operations  1.3 us (1%)
    pallas_call x1, Pallas kernels, on_device(): pl.pallas_call(kernel, out_shape=(jax.ShapeDtypeStruct((16, D), bf16), ja...  96.8 us
    unnamed x4, local copies, waits for them, and re-layouts  2.27 us

profile of v4, /device:TPU:1, one launch (start us, length us, event | category | flops | bytes accessed | tf_op | source)
XLA Modules:
  0.0 100.4 jit_solution(11952655008330409497)
XLA Ops:
  1.3 96.8 %sublayer.1 = (bf16[16,5376]{1,0:T(8,128)(2,1)}, bf16[8,5376]{1,0:T(8,128)(2,1)}) custom-call(bf16[16,5376]{1,0:T(8,128)(2,1)} %prompt.1, bf16[8,5376]{1,0:T(8,128)(2,1)} %bitcast.5, s32[1]{0:T(128)S(6)} %copy.15.lens, f32[5376]{0:T(1024)} %in_gain.1, bf16[168,512]{1,0:T(8,128)(2,1)} %wq.1, bf16[168,256]{1,0:T(8,128)(2,1)} %wk.1, bf16[168,256]{1,0:T(8,128)(2,1)} %wv.1, ...), custom_call_target="tpu_custom_call" | custom-call | tf_op jit(solution)/shard_map/sublayer/pallas_call | solution.py:616
  98.1 0.0 copy-start
  98.1 1.6 %copy.16 = bf16[16,5376]{1,0:T(8,128)(2,1)} copy(bf16[16,5376]{1,0:T(8,128)(2,1)} %get-tuple-element.8) | data formatting | bytes 344064
  99.8 0.0 copy-done
  99.8 0.6 copy.17
Async XLA Ops:
  98.1 1.6 %copy-start = (bf16[8,5376]{1,0:T(8,128)(2,1)S(1)}, bf16[8,5376]{1,0:T(8,128)(2,1)}, u32[]{:S(2)}) copy-start(bf16[8,5376]{1,0:T(8,128)(2,1)} %get-tuple-element.5) | copy-start | bytes 258052

commit v5 on v4

--- a/solution.py
+++ b/solution.py
@@ -366,6 +366,16 @@
                 one(0, 0)
 
             one(1, (z + 8 - k) // 8)
+
+    def window_step(dz):
+        zz = (z + dz) % 8
+
+        @pl.when(zz >= 4)
+        def _():
+            pair = kvg[1, zz].reshape(256, 256)
+            weights = scored(qa[...], pair[:, :128])
+            seen = col + 64 * (zz - 4) > row % 64
+            add_in(2, jnp.where(seen, weights, 0.0), pair[:, 128:])
 
     exchange(0)
     og[z * 2 + c] = wo[...]
@@ -445,15 +455,12 @@
     add_in(2, jnp.where(own_seen, own, 0.0), akv[:, 128:])
     kv_done(3)
     prompt_step(3)
+    for dz in (0, 1, 2, 3, 5, 6, 7):
+        window_step(dz)
     kv_step(4)
     kv_done(4)
     prompt_step(4)
-    for zz in range(4, 8):
-        pair = kvg[1, zz].reshape(256, 256)
-        weights = scored(qa[...], pair[:, :128])
-        if zz == 4:
-            weights = jnp.where(col > row % 64, weights, 0.0)
-        add_in(2, weights, pair[:, 128:])
+    window_step(4)
 
 
     for g in range(2):

time: 101 us -> 102 us (level)
  Pallas kernels: 96.8 us -> 98 us
    pallas_call x1, Pallas kernels: 96.8 us -> 98 us  [on_device(): pl.pallas_call(kernel, out_shape=(jax.ShapeDtypeStruct((16, D), bf16), ja...]
where the time goes in v5:
time: 102 us
  Pallas kernels  98 us (96%)
  local copies, waits for them, and re-layouts  2.27 us (2%)
  between operations  1.3 us (1%)
    pallas_call x1, Pallas kernels, on_device(): pl.pallas_call(kernel, out_shape=(jax.ShapeDtypeStruct((16, D), bf16), ja...  98 us
    unnamed x4, local copies, waits for them, and re-layouts  2.27 us

profile of v5, /device:TPU:1, one launch (start us, length us, event | category | flops | bytes accessed | tf_op | source)
XLA Modules:
  0.0 101.6 jit_solution(16297880417285662883)
XLA Ops:
  1.3 98.0 %sublayer.1 = (bf16[16,5376]{1,0:T(8,128)(2,1)}, bf16[8,5376]{1,0:T(8,128)(2,1)}) custom-call(bf16[16,5376]{1,0:T(8,128)(2,1)} %prompt.1, bf16[8,5376]{1,0:T(8,128)(2,1)} %bitcast.5, s32[1]{0:T(128)S(6)} %copy.15.lens, f32[5376]{0:T(1024)} %in_gain.1, bf16[168,512]{1,0:T(8,128)(2,1)} %wq.1, bf16[168,256]{1,0:T(8,128)(2,1)} %wk.1, bf16[168,256]{1,0:T(8,128)(2,1)} %wv.1, ...), custom_call_target="tpu_custom_call" | custom-call | tf_op jit(solution)/shard_map/sublayer/pallas_call | solution.py:623
  99.3 0.0 copy-start
  99.3 1.6 %copy.16 = bf16[16,5376]{1,0:T(8,128)(2,1)} copy(bf16[16,5376]{1,0:T(8,128)(2,1)} %get-tuple-element.8) | data formatting | bytes 344064
  100.9 0.0 copy-done
  100.9 0.6 copy.17
Async XLA Ops:
  99.3 1.6 %copy-start = (bf16[8,5376]{1,0:T(8,128)(2,1)S(1)}, bf16[8,5376]{1,0:T(8,128)(2,1)}, u32[]{:S(2)}) copy-start(bf16[8,5376]{1,0:T(8,128)(2,1)} %get-tuple-element.5) | copy-start | bytes 258052
